TPU v7x, 512 devices: a whole 4x8x8 slice. The times are simulated.
512 devices in a mesh: row: 32 (over z, x_lo, core), col: 16 (over x_hi, y).
Axes of the slice: x: 4 (x_hi: 2, x_lo: 2; x = x_hi * 2 + x_lo), y: 8, z: 8, core: 2. Of those that a mesh axis runs over, the one named last changes fastest.
Arguments:
- right_side: float32 [1, 32, 1024, 512], P(None, 'row', 'col'), may hold values from -6 to 6
- prior_panel: bfloat16 [1, 32, 1, 16, 1024, 1024], P(None, 'row', None, 'col'), may hold values from -0.0625 to 0.0625
- prior_solved: bfloat16 [1, 16, 1024, 512], P(None, 'col'), may hold values from -6 to 6
- window_panel: bfloat16 [1, 32, 4, 1024, 1024], P(None, 'row', None, 'col'), may hold values from -0.09375 to 0.09375
- diag_inverse: bfloat16 [4, 1024, 1024], P(None, 'col'), as said below
Outputs:
- updated: float32 [1, 32, 1024, 512], P(None, 'row', 'col')
Inputs may be any that keep to these rules, and one draw needn't show every extreme that they name: `diag_inverse`: lower triangular: entries above the diagonal of each block are zero; diagonal entries are positive.
All inputs are finite; a program needn't handle non-finite values.
Results may differ from a plain program's by a relative error of at most 0.022.
Values may be sent and summed in bfloat16 or wider, within the bound.
A program may use at most 128 MiB of HBM per device.

v0:
```python
import jax
import jax.numpy as jnp
from jax import lax
from jax.sharding import PartitionSpec as P


def broadcast(value, axis, source):
    kept = jnp.where(lax.axis_index(axis) == source, value, 0).astype(value.dtype)
    return lax.psum(kept, axis)


def per_device(right_side, prior_panel, prior_solved, window_panel, diag_inverse):
    rows_each = right_side.shape[0]
    slice_rows = right_side.shape[2]
    columns = right_side.shape[3]
    prior_each = prior_panel.shape[2]
    block_size = prior_panel.shape[4]
    tick_count = window_panel.shape[2]
    row_count = lax.axis_size("row")
    panel = prior_panel.reshape(rows_each, prior_each, block_size, block_size)
    solved_here = prior_solved.reshape(prior_each, block_size, columns)
    prior = lax.psum_scatter(
        jnp.einsum("tpxj,pjn->xtn", panel, solved_here, preferred_element_type=jnp.float32).astype(
            jnp.bfloat16
        ),
        "col",
        scatter_dimension=0,
        tiled=True,
    ).astype(jnp.float32)
    prior = jnp.transpose(prior, (1, 0, 2))
    pending = right_side[:, 0] - prior
    window = window_panel.reshape(rows_each, tick_count, slice_rows, block_size)
    row_here = lax.axis_index("row")
    block_ids = jnp.arange(rows_each, dtype=jnp.int32) * row_count + row_here
    solved_list = []
    for tick_index in range(tick_count):
        head_rows = pending[0].astype(jnp.bfloat16)
        waiting = lax.all_gather(head_rows, "col", axis=0, tiled=True)
        window_tick = window[:, tick_index]
        mine = jnp.dot(
            diag_inverse[tick_index], waiting, preferred_element_type=jnp.float32
        ).astype(jnp.bfloat16)
        mine = broadcast(mine, "row", tick_index)
        update = jnp.einsum(
            "txj,jn->txn",
            window_tick,
            lax.all_gather(mine, "col", axis=0, tiled=True),
            preferred_element_type=jnp.float32,
        )
        live = block_ids > tick_index
        pending = pending - jnp.where(live[:, None, None], update, jnp.float32(0.0))
        solved_list.append(mine)
    stacked = jnp.stack(solved_list, axis=0)
    chosen = lax.dynamic_index_in_dim(
        stacked, jnp.minimum(row_here, tick_count - 1), 0, keepdims=False
    )
    first_row = jnp.where(row_here < tick_count, chosen.astype(jnp.float32), pending[0])
    pending = pending.at[0].set(first_row)
    return pending[:, None]


def solution(mesh):
    return jax.shard_map(
        per_device,
        mesh=mesh,
        in_specs=(
            P(None, "row", "col", None),
            P(None, "row", None, "col", None, None),
            P(None, "col", None, None),
            P(None, "row", None, "col", None),
            P(None, "col", None),
        ),
        out_specs=P(None, "row", "col", None),
        check_vma=False,
    )
```

profile of v0, /device:TPU:1, one launch (start us, length us, event | category | flops | bytes accessed | tf_op | source)
XLA Modules:
  0.0 1704.9 jit_solution(634280949930361512)
XLA Ops:
  6.5 1.6 copy-done
  8.1 2.5 fusion.5
  10.7 1.3 copy.19
  12.0 0.0 all-gather.9.cloned.1.call-start
  12.1 204.9 %reduce-scatter.4.cloned.1.call-done = bf16[64,512]{1,0:T(8,128)(2,1)} async-done(((bf16[1024,512]{1,0:T(8,128)(2,1)}), bf16[64,512]{1,0:T(8,128)(2,1)}) %reduce-scatter.4.cloned.1.call-update) | async-done | bytes 65552
  216.9 1.0 copy.20
  217.9 0.1 copy.16
  218.0 0.6 fusion.35
  218.7 0.0 all-gather.9.cloned.1.call-update
  218.7 0.0 all-reduce.5.cloned.1.call-start
  218.8 85.3 %all-gather.9.cloned.1.call-done = bf16[1024,512]{1,0:T(8,128)(2,1)} async-done(((bf16[64,512]{1,0:T(8,128)(2,1)}), bf16[1024,512]{1,0:T(8,128)(2,1)}) %all-gather.9.cloned.1.call-update) | async-done | bytes 1048592 | tf_op jit(solution)/shard_map/all_gather | solution.py:38
  304.0 2.2 fusion.19
  306.3 0.0 all-gather.11.cloned.1.call-start
  306.3 200.1 %all-reduce.5.cloned.1.call-done = bf16[64,512]{1,0:T(8,128)(2,1)} async-done(((bf16[64,512]{1,0:T(8,128)(2,1)}), bf16[64,512]{1,0:T(8,128)(2,1)}) %all-reduce.5.cloned.1.call-update) | async-done | bytes 65552 | tf_op jit(solution)/shard_map/psum | solution.py:9
  506.4 0.0 all-gather.11.cloned.1.call-update
  506.4 0.0 all-gather.13.cloned.1.call-start
  506.4 82.4 %all-gather.11.cloned.1.call-done = bf16[1024,512]{1,0:T(8,128)(2,1)} async-done(((bf16[64,512]{1,0:T(8,128)(2,1)}), bf16[1024,512]{1,0:T(8,128)(2,1)}) %all-gather.11.cloned.1.call-update) | async-done | bytes 1048592 | tf_op jit(solution)/shard_map/all_gather | solution.py:47
  588.8 2.2 fusion.40
  591.0 0.0 all-gather.13.cloned.1.call-update
  591.1 0.0 all-reduce.7.cloned.1.call-start
  591.1 82.2 %all-gather.13.cloned.1.call-done = bf16[1024,512]{1,0:T(8,128)(2,1)} async-done(((bf16[64,512]{1,0:T(8,128)(2,1)}), bf16[1024,512]{1,0:T(8,128)(2,1)}) %all-gather.13.cloned.1.call-update) | async-done | bytes 1048592 | tf_op jit(solution)/shard_map/all_gather | solution.py:38
  673.3 2.2 fusion.21
  675.5 0.0 all-reduce.7.cloned.1.call-update
  675.5 0.0 all-gather.15.cloned.1.call-start
  675.5 200.3 %all-reduce.7.cloned.1.call-done = bf16[64,512]{1,0:T(8,128)(2,1)} async-done(((bf16[64,512]{1,0:T(8,128)(2,1)}), bf16[64,512]{1,0:T(8,128)(2,1)}) %all-reduce.7.cloned.1.call-update) | async-done | bytes 65552 | tf_op jit(solution)/shard_map/psum | solution.py:9
  875.8 0.0 all-gather.15.cloned.1.call-update
  875.8 0.0 all-gather.17.cloned.1.call-start
  875.9 82.0 %all-gather.15.cloned.1.call-done = bf16[1024,512]{1,0:T(8,128)(2,1)} async-done(((bf16[64,512]{1,0:T(8,128)(2,1)}), bf16[1024,512]{1,0:T(8,128)(2,1)}) %all-gather.15.cloned.1.call-update) | async-done | bytes 1048592 | tf_op jit(solution)/shard_map/all_gather | solution.py:47
  957.9 2.2 fusion.41
  960.1 0.0 all-gather.17.cloned.1.call-update
  960.2 0.0 all-reduce.9.cloned.1.call-start
  960.2 81.8 %all-gather.17.cloned.1.call-done = bf16[1024,512]{1,0:T(8,128)(2,1)} async-done(((bf16[64,512]{1,0:T(8,128)(2,1)}), bf16[1024,512]{1,0:T(8,128)(2,1)}) %all-gather.17.cloned.1.call-update) | async-done | bytes 1048592 | tf_op jit(solution)/shard_map/all_gather | solution.py:38
  1042.1 2.2 fusion.23
  1044.2 0.0 all-reduce.9.cloned.1.call-update
  1044.2 0.0 all-gather.19.cloned.1.call-start
  1044.3 200.1 %all-reduce.9.cloned.1.call-done = bf16[64,512]{1,0:T(8,128)(2,1)} async-done(((bf16[64,512]{1,0:T(8,128)(2,1)}), bf16[64,512]{1,0:T(8,128)(2,1)}) %all-reduce.9.cloned.1.call-update) | async-done | bytes 65552 | tf_op jit(solution)/shard_map/psum | solution.py:9
  1244.5 0.0 all-gather.21.cloned.1.call-start
  1244.5 82.4 %all-gather.19.cloned.1.call-done = bf16[1024,512]{1,0:T(8,128)(2,1)} async-done(((bf16[64,512]{1,0:T(8,128)(2,1)}), bf16[1024,512]{1,0:T(8,128)(2,1)}) %all-gather.19.cloned.1.call-update) | async-done | bytes 1048592 | tf_op jit(solution)/shard_map/all_gather | solution.py:47
  1326.9 2.2 fusion.42
  1329.0 0.0 all-gather.21.cloned.1.call-update
  1329.1 0.0 all-reduce.11.cloned.1.call-start
  1329.1 82.4 %all-gather.21.cloned.1.call-done = bf16[1024,512]{1,0:T(8,128)(2,1)} async-done(((bf16[64,512]{1,0:T(8,128)(2,1)}), bf16[1024,512]{1,0:T(8,128)(2,1)}) %all-gather.21.cloned.1.call-update) | async-done | bytes 1048592 | tf_op jit(solution)/shard_map/all_gather | solution.py:38
  1411.5 2.2 fusion.25
  1413.7 0.0 all-reduce.11.cloned.1.call-update
  1413.7 0.0 all-gather.23.cloned.1.call-start
  1413.7 200.3 %all-reduce.11.cloned.1.call-done = bf16[64,512]{1,0:T(8,128)(2,1)} async-done(((bf16[64,512]{1,0:T(8,128)(2,1)}), bf16[64,512]{1,0:T(8,128)(2,1)}) %all-reduce.11.cloned.1.call-update) | async-done | bytes 65552 | tf_op jit(solution)/shard_map/psum | solution.py:9
  1614.0 82.1 %all-gather.23.cloned.1.call-done = bf16[1024,512]{1,0:T(8,128)(2,1)} async-done(((bf16[64,512]{1,0:T(8,128)(2,1)}), bf16[1024,512]{1,0:T(8,128)(2,1)}) %all-gather.23.cloned.1.call-update) | async-done | bytes 1048592 | tf_op jit(solution)/shard_map/all_gather | solution.py:47
  1696.1 2.2 fusion.11
  (16 shorter events, 0.1 us)
Async XLA Ops:
  6.5 1.6 copy-start
  6.5 210.4 %reduce-scatter.4.cloned.1.call-start = ((), (), s32[]{:S(2)}) async-start(), calls=%async_computation.13 | async-start | bytes 1114112
  10.7 207.4 %copy-start.2 = (f32[1,1,64,512]{3,2,1,0:T(8,128)S(1)}, f32[1,1,64,512]{3,2,1,0:T(8,128)}, u32[]{:S(2)}) copy-start(f32[1,1,64,512]{3,2,1,0:T(8,128)} %param.7) | copy-start | bytes 393220
  12.0 661.3 %copy-start.1 = (bf16[4,64,1024]{2,1,0:T(8,128)(2,1)S(1)}, bf16[4,64,1024]{2,1,0:T(8,128)(2,1)}, u32[]{:S(2)}) copy-start(bf16[4,64,1024]{2,1,0:T(8,128)(2,1)} %param.11) | copy-start | bytes 1572868
  12.0 292.0 %all-gather.9.cloned.1.call-start = ((), (), s32[]{:S(2)}) async-start(), calls=%async_computation.1 | async-start | bytes 1114112 | tf_op jit(solution)/shard_map/all_gather | solution.py:38
  218.7 287.7 %all-reduce.5.cloned.1.call-start = ((), (), s32[]{:S(2)}) async-start(), calls=%async_computation.2 | async-start | bytes 131072 | tf_op jit(solution)/shard_map/psum | solution.py:9
  306.3 282.6 %all-gather.11.cloned.1.call-start = ((), (), s32[]{:S(2)}) async-start(), calls=%async_computation.3 | async-start | bytes 1114112 | tf_op jit(solution)/shard_map/all_gather | solution.py:47
  506.4 166.9 %all-gather.13.cloned.1.call-start = ((), (), s32[]{:S(2)}) async-start(), calls=%async_computation.4 | async-start | bytes 1114112 | tf_op jit(solution)/shard_map/all_gather | solution.py:38
  591.1 284.7 %all-reduce.7.cloned.1.call-start = ((), (), s32[]{:S(2)}) async-start(), calls=%async_computation.5 | async-start | bytes 131072 | tf_op jit(solution)/shard_map/psum | solution.py:9
  591.1 735.8 %copy-start.3 = (bf16[1,1,4,64,1024]{4,3,2,1,0:T(8,128)(2,1)S(1)}, bf16[1,1,4,64,1024]{4,3,2,1,0:T(8,128)(2,1)}, u32[]{:S(2)}) copy-start(bf16[1,1,4,64,1024]{4,3,2,1,0:T(8,128)(2,1)} %param.10) | copy-start | bytes 1572868
  675.5 282.4 %all-gather.15.cloned.1.call-start = ((), (), s32[]{:S(2)}) async-start(), calls=%async_computation.6 | async-start | bytes 1114112 | tf_op jit(solution)/shard_map/all_gather | solution.py:47
  875.8 166.3 %all-gather.17.cloned.1.call-start = ((), (), s32[]{:S(2)}) async-start(), calls=%async_computation.7 | async-start | bytes 1114112 | tf_op jit(solution)/shard_map/all_gather | solution.py:38
  960.2 284.3 %all-reduce.9.cloned.1.call-start = ((), (), s32[]{:S(2)}) async-start(), calls=%async_computation.8 | async-start | bytes 131072 | tf_op jit(solution)/shard_map/psum | solution.py:9
  960.2 735.9 %copy-start.4 = (bf16[64,512]{1,0:T(8,128)(2,1)S(1)}, bf16[64,512]{1,0:T(8,128)(2,1)}, u32[]{:S(2)}) copy-start(bf16[64,512]{1,0:T(8,128)(2,1)} %all-reduce.5.cloned.1.call-done) | copy-start | bytes 196612
  960.2 735.9 %copy-start.5 = (bf16[64,512]{1,0:T(8,128)(2,1)S(1)}, bf16[64,512]{1,0:T(8,128)(2,1)}, u32[]{:S(2)}) copy-start(bf16[64,512]{1,0:T(8,128)(2,1)} %all-reduce.7.cloned.1.call-done) | copy-start | bytes 196612
  1044.2 282.6 %all-gather.19.cloned.1.call-start = ((), (), s32[]{:S(2)}) async-start(), calls=%async_computation.9 | async-start | bytes 1114112 | tf_op jit(solution)/shard_map/all_gather | solution.py:47
  1244.5 167.1 %all-gather.21.cloned.1.call-start = ((), (), s32[]{:S(2)}) async-start(), calls=%async_computation.10 | async-start | bytes 1114112 | tf_op jit(solution)/shard_map/all_gather | solution.py:38
  1329.1 285.0 %all-reduce.11.cloned.1.call-start = ((), (), s32[]{:S(2)}) async-start(), calls=%async_computation.11 | async-start | bytes 131072 | tf_op jit(solution)/shard_map/psum | solution.py:9
  1413.7 282.4 %all-gather.23.cloned.1.call-start = ((), (), s32[]{:S(2)}) async-start(), calls=%async_computation.12 | async-start | bytes 1114112 | tf_op jit(solution)/shard_map/all_gather | solution.py:47
Sparse Core Ops, SparseCore 0:
  12.2 204.7 reduce-scatter.3
  220.1 83.8 all-gather.8
  306.9 199.3 all-reduce.4
  509.9 78.9 all-gather.10
  592.3 80.9 all-gather.12
  676.3 199.4 all-reduce.6
  879.0 78.9 all-gather.14
  961.1 80.9 all-gather.16
  1045.0 199.3 all-reduce.8
  1247.9 78.9 all-gather.18
  1330.5 80.9 all-gather.20
  1414.5 199.4 all-reduce.10
  1617.2 78.9 all-gather.22
where the time goes:
time: 1710 us; the launch traced here: 1700 us
  waiting for transfers between devices  1670 us (98%)
  matrix products  20 us (1%)
    psum x4, waiting for transfers between devices, broadcast(): return lax.psum(kept, axis)  801 us
    all_gather x4, waiting for transfers between devices, per_device(): waiting = lax.all_gather(head_rows, 'col', axis=0, tiled=True)  332 us
    all_gather x4, waiting for transfers between devices, per_device(): lax.all_gather(mine, 'col', axis=0, tiled=True)  329 us
    unnamed x14, waiting for transfers between devices  205 us
  transfers between devices with their start and end apart: 13, of which 13 were waited for; matrix products, arithmetic and copies ran while one was open for 0% of the time, Pallas kernels for 0%

commit v1 on v0

v1 whole, which is shorter than its diff:
```python
import functools

import jax
import jax.numpy as jnp
from jax import lax
from jax.experimental import pallas as pl
from jax.experimental.pallas import tpu as pltpu
from jax.sharding import PartitionSpec as P

MESH = pl.DeviceIdType.MESH
F32 = jnp.float32
BF16 = jnp.bfloat16
LEVEL = 4
LANES = 128


def nt_dot(a, b):
    return lax.dot_general(
        a, b, (((1,), (1,)), ((), ())), preferred_element_type=F32
    )


def kernel(
    nz,
    ncol,
    rhs_h,
    panel_h,
    prior_h,
    win_h,
    dinv_h,
    out_ref,
    rhs,
    panel,
    prior,
    win,
    dinv,
    sendb,
    recv1,
    pend,
    pt,
    sca,
    pin,
    acc,
    a1,
    a2,
    sz,
    wsrc,
    wl,
    wc,
    usum,
    ub,
    load_sem,
    rs_send,
    rs_recv,
    sa_send,
    sa_recv,
    sb_send,
    sb_recv,
    wr_send,
    wr_recv,
    wc_send,
    wc_recv,
    wl_send,
    wl_recv,
    a1_send,
    a1_recv,
    a2_send,
    a2_recv,
    z_send,
    z_recv,
    u_send,
    u_recv,
):
    row = lax.axis_index("row")
    col = lax.axis_index("col")
    zed = row // LEVEL
    cls = row % LEVEL
    ticks, rows, size = win.shape
    width = pin.shape[1]
    columns = rhs.shape[1]
    parity = col % 2

    loads = [
        pltpu.make_async_copy(src, dst, load_sem.at[i])
        for i, (src, dst) in enumerate(
            ((prior_h, prior), (panel_h, panel), (win_h, win), (dinv_h, dinv), (rhs_h, rhs))
        )
    ]
    for load in loads:
        load.start()

    def on_col(d):
        return (row, lax.rem(col + d, ncol))

    def on_z(d):
        return (lax.rem(zed + d, nz) * LEVEL + cls, col)

    def on_level(d):
        return (zed * LEVEL + lax.rem(cls + d, LEVEL), col)

    def remote(src, dst, send, recv, device):
        return pltpu.make_async_remote_copy(
            src_ref=src,
            dst_ref=dst,
            send_sem=send,
            recv_sem=recv,
            device_id=device,
            device_id_type=MESH,
        )

    def wait_for(ref, sem):
        pltpu.make_async_copy(ref, ref, sem).wait()

    barrier = pltpu.get_barrier_semaphore()

    def greet(where):
        def body(d, carry):
            pl.semaphore_signal(
                barrier, inc=1, device_id=where(d), device_id_type=MESH
            )
            return carry

        return body

    lax.fori_loop(1, ncol, greet(on_col), 0)
    lax.fori_loop(1, nz, greet(on_z), 0)
    lax.fori_loop(1, LEVEL, greet(on_level), 0)
    pl.semaphore_wait(barrier, (ncol - 1) + (nz - 1) + (LEVEL - 1))

    mine = jnp.maximum(cls - 1, 0)
    loads[2].wait()

    def relay(j, device):
        return remote(wc.at[mine, j], wc.at[mine, j], wr_send, wr_recv.at[j], device)

    half = nz // 2
    upward = (zed < half)
    downward = (zed == 0) | (zed > half + 1)
    for j in range(LEVEL - 1):

        @pl.when((j < cls) & (zed == 0))
        def _():
            wc[mine, j] = win[j]
            relay(j, on_z(1)).start()
            if nz > 2:
                relay(j, on_z(nz - 1)).start()

    loads[0].wait()
    loads[1].wait()
    per_block = 4 if ncol % 4 == 0 else ncol
    blocks = ncol // per_block
    first = col // per_block + 1

    def product(i, carry):
        block = lax.rem(first + i, blocks)
        start = pl.multiple_of(block * per_block * rows, per_block * rows)
        part = jnp.dot(
            panel[pl.ds(start, per_block * rows), :], prior[...], preferred_element_type=F32
        ).astype(BF16)
        for s in range(per_block):
            sendb[block * per_block + s] = part[s * rows : (s + 1) * rows]

        def send(s, inner):
            target = block * per_block + s

            @pl.when(target != col)
            def _():
                slot = lax.rem(target - col + ncol, ncol) - 1
                remote(
                    sendb.at[target], recv1.at[slot], rs_send, rs_recv, (row, target)
                ).start()

            return inner

        return lax.fori_loop(0, per_block, send, carry)

    lax.fori_loop(0, blocks, product, 0)

    for j in range(LEVEL - 1):

        @pl.when((j < cls) & (zed > 0))
        def _():
            wait_for(wc.at[mine, j], wr_recv.at[j])

        @pl.when((j < cls) & (zed > 0) & upward)
        def _():
            relay(j, on_z(1)).start()

        @pl.when((j < cls) & (zed > 0) & downward)
        def _():
            relay(j, on_z(nz - 1)).start()

        @pl.when(j < cls)
        def _():
            def share(d, carry):
                remote(
                    wc.at[mine, j], wc.at[mine, j], wc_send, wc_recv.at[mine, j], on_level(d)
                ).start()
                return carry

            lax.fori_loop(1, LEVEL, share, 0)

    @pl.when(zed == 0)
    def _():
        picks = (
            lax.broadcasted_iota(jnp.int32, (rows, size), 1)
            == lax.broadcasted_iota(jnp.int32, (rows, size), 0) + col * rows
        )
        for k in range(ticks):
            wsrc[k] = jnp.where(picks & (cls == k), 1.0, 0.0).astype(BF16)

    @pl.when(zed > 0)
    def _():
        wsrc[...] = win[...]

    def spread(d, carry):
        remote(wsrc, wl.at[:, cls], wl_send, wl_recv, on_level(d)).start()
        return carry

    lax.fori_loop(1, LEVEL, spread, 0)
    wl[:, cls] = wsrc[...]

    loads[4].wait()
    loads[3].wait()
    wait_for(recv1, rs_recv)
    total = sendb[col].astype(F32)
    for s in range(ncol - 1):
        total = total + recv1[s].astype(F32)
    pend[...] = rhs[...] - total

    @pl.when(zed == 0)
    def _():
        value = pend[...]
        for q in range(LEVEL):
            part = jnp.concatenate(
                [value[:, q * LANES : (q + 1) * LANES]] * 2, axis=0
            ).T.astype(BF16)
            for t in range(nz):
                pt[q, t] = part[t * width : (t + 1) * width]

        def send(d, carry):
            remote(pt.at[:, lax.rem(zed + d, nz)], sca, sa_send, sa_recv, on_z(d)).start()
            return carry

        lax.fori_loop(1, nz, send, 0)
        sca[...] = pt[:, 0]

    @pl.when(zed > 0)
    def _():
        wait_for(sca, sa_recv)

    def deal(d, carry):
        remote(
            sca.at[lax.rem(cls + d, LEVEL)], pin.at[cls], sb_send, sb_recv, on_level(d)
        ).start()
        return carry

    lax.fori_loop(1, LEVEL, deal, 0)
    pin[cls] = sca[cls]
    wait_for(pin.at[pl.ds(0, LEVEL - 1)], sb_recv)
    for k in range(ticks):
        acc[k] = pin[k].astype(F32)

    lane = lax.broadcasted_iota(jnp.int32, (width, LANES), 1)
    kept = (lane >= parity * rows) & (lane < parity * rows + rows)

    def twice(value):
        return jnp.concatenate([value, value], axis=1)

    def gather(buf, k, value, send, recv):
        buf[k, col] = jnp.where(kept, value, 0.0).astype(BF16)

        def body(d, carry):
            remote(buf.at[k, col], buf.at[k, col], send.at[k], recv.at[k], on_col(d)).start()
            return carry

        lax.fori_loop(1, ncol, body, 0)

    def whole(buf, k, recv):
        wait_for(buf.at[k, pl.ds(0, ncol - 1)], recv.at[k])
        return jnp.concatenate(
            [buf[k, 2 * p] + buf[k, 2 * p + 1] for p in range(ncol // 2)], axis=1
        )

    def update_row(k, later, solved):
        @pl.when(cls != later)
        def _():
            wait_for(wc.at[later - 1, k], wc_recv.at[later - 1, k])

        acc[later] = acc[later] - twice(nt_dot(solved, wc[later - 1, k]))

    def final(k):
        if k == 0:
            wait_for(wl.at[:, pl.ds(0, LEVEL - 1)], wl_recv)
        if nz > 1:
            wait_for(sz.at[k, pl.ds(0, (nz - 1) * width)], z_recv.at[k])
        part = nt_dot(wl[k].reshape(LEVEL * rows, size), sz[k])
        for q in range(LEVEL):
            piece = part[q * rows : (q + 1) * rows]
            usum[q] = piece if k == 0 else usum[q] + piece

    place = pl.multiple_of(zed * width, width)
    solved = None
    for k in range(ticks):
        gather(a1, k, acc[k], a1_send, a1_recv)
        if k > 0:
            for later in range(k + 1, ticks):
                update_row(k - 1, later, solved)
        waiting = whole(a1, k, a1_recv)
        gather(a2, k, twice(nt_dot(waiting, dinv[k])), a2_send, a2_recv)
        if k >= 2:
            final(k - 2)
        solved = whole(a2, k, a2_recv)
        sz[k, pl.ds(place, width), :] = solved

        def along(d, carry):
            part = sz.at[k, pl.ds(place, width), :]
            remote(part, part, z_send, z_recv.at[k], on_z(d)).start()
            return carry

        lax.fori_loop(1, nz, along, 0)
        if k + 1 < ticks:
            update_row(k, k + 1, solved)

    for k in range(max(ticks - 2, 0), ticks):
        final(k)

    def give(d, carry):
        remote(
            usum.at[lax.rem(cls + d, LEVEL)], ub.at[cls], u_send, u_recv, on_level(d)
        ).start()
        return carry

    lax.fori_loop(1, LEVEL, give, 0)
    ub[cls] = usum[cls]
    wait_for(ub.at[pl.ds(0, LEVEL - 1)], u_recv)
    for q in range(LEVEL):
        cut = slice(q * LANES, (q + 1) * LANES)
        out_ref[:, cut] = jnp.where(zed == 0, ub[q], pend[:, cut] - ub[q])

    wait_for(recv1, rs_send)
    wait_for(ub.at[pl.ds(0, LEVEL - 1)], u_send)
    wait_for(pin.at[pl.ds(0, LEVEL - 1)], sb_send)
    wait_for(wl.at[:, pl.ds(0, LEVEL - 1)], wl_send)
    for k in range(ticks):
        wait_for(a1.at[k, pl.ds(0, ncol - 1)], a1_send.at[k])
        wait_for(a2.at[k, pl.ds(0, ncol - 1)], a2_send.at[k])
        wait_for(sz.at[k, pl.ds(0, (nz - 1) * width)], z_send)

    @pl.when(zed == 0)
    def _():
        wait_for(pt.at[:, pl.ds(0, nz - 1)], sa_send)

    for j in range(LEVEL - 1):

        @pl.when((j < cls) & upward)
        def _():
            wait_for(wc.at[mine, j], wr_send)

        @pl.when((j < cls) & downward & (nz > 2))
        def _():
            wait_for(wc.at[mine, j], wr_send)

        @pl.when(j < cls)
        def _():
            wait_for(wc.at[pl.ds(0, LEVEL - 1), j], wc_send)


def per_device(right_side, prior_panel, prior_solved, window_panel, diag_inverse):
    rows, columns = right_side.shape[2:]
    size = prior_panel.shape[4]
    ticks = window_panel.shape[2]
    ncol = lax.axis_size("col")
    nz = lax.axis_size("row") // LEVEL
    width = LANES // nz
    dma = pltpu.SemaphoreType.DMA
    vmem = pltpu.VMEM
    out = pl.pallas_call(
        functools.partial(kernel, nz, ncol),
        out_shape=jax.ShapeDtypeStruct((rows, columns), F32),
        in_specs=[pl.BlockSpec(memory_space=pl.ANY)] * 5,
        out_specs=pl.BlockSpec(memory_space=pltpu.VMEM),
        scratch_shapes=[
            vmem((rows, columns), F32),
            vmem((size, size), BF16),
            vmem((size, columns), BF16),
            vmem((ticks, rows, size), BF16),
            vmem((ticks, rows, size), BF16),
            vmem((ncol, rows, columns), BF16),
            vmem((ncol - 1, rows, columns), BF16),
            vmem((rows, columns), F32),
            vmem((LEVEL, nz, width, LANES), BF16),
            vmem((LEVEL, width, LANES), BF16),
            vmem((LEVEL, width, LANES), BF16),
            vmem((ticks, width, LANES), F32),
            vmem((ticks, ncol, width, LANES), BF16),
            vmem((ticks, ncol, width, LANES), BF16),
            vmem((ticks, LANES, size), BF16),
            vmem((ticks, rows, size), BF16),
            vmem((ticks, LEVEL, rows, size), BF16),
            vmem((LEVEL - 1, LEVEL - 1, rows, size), BF16),
            vmem((LEVEL, rows, LANES), F32),
            vmem((LEVEL, rows, LANES), F32),
            dma((5,)),
            dma,
            dma,
            dma,
            dma,
            dma,
            dma,
            dma,
            dma((LEVEL - 1,)),
            dma,
            dma((LEVEL - 1, LEVEL - 1)),
            dma,
            dma,
            dma((ticks,)),
            dma((ticks,)),
            dma((ticks,)),
            dma((ticks,)),
            dma,
            dma((ticks,)),
            dma,
            dma,
        ],
        compiler_params=pltpu.CompilerParams(
            collective_id=0,
            has_side_effects=True,
            vmem_limit_bytes=40 * 1024 * 1024,
        ),
    )(
        right_side.reshape(rows, columns),
        prior_panel.reshape(size, size),
        prior_solved.reshape(size, columns),
        window_panel.reshape(ticks, rows, size),
        diag_inverse,
    )
    return out.reshape(right_side.shape)


def solution(mesh):
    return jax.shard_map(
        per_device,
        mesh=mesh,
        in_specs=(
            P(None, "row", "col", None),
            P(None, "row", None, "col", None, None),
            P(None, "col", None, None),
            P(None, "row", None, "col", None),
            P(None, "col", None),
        ),
        out_specs=P(None, "row", "col", None),
        check_vma=False,
    )
```

time: 1710 us -> 140 us (0.08)
  waiting for transfers between devices: 1670 us -> 0 us
  Pallas kernels: 0 us -> 133 us
  matrix products: 20 us -> 0 us
    psum x4 -> x0, waiting for transfers between devices: 801 us -> none  [broadcast(): return lax.psum(kept, axis)]
    all_gather x8 -> x0, waiting for transfers between devices: 661 us -> none  [the longest x4 332 us: per_device(): waiting = lax.all_gather(head_rows, 'col', axis=0, tiled=True)]
    unnamed x14 -> x0, waiting for transfers between devices: 205 us -> none
    pallas_call x0 -> x1, Pallas kernels: none -> 133 us  [per_device(): pl.pallas_call(functools.partial(kernel, nz, ncol), out_shape=jax.ShapeDt...]
    dot_general x9 -> x0, matrix products: 20 us -> none  [the longest x4 8.81 us: per_device(): jnp.einsum('txj,jn->txn', window_tick, lax.all_gather(mine, 'col', axis=0...]
  transfers between devices with their start and end apart: 13 -> 0, of which waited for: 13 -> 0; matrix products, arithmetic and copies ran while one was open for 0% -> 0% of each run, Pallas kernels for 0% -> 0%
where the time goes in v1:
time: 140 us; the launch traced here: 139 us
  Pallas kernels  133 us (95%)
  local copies, waits for them, and re-layouts  6.46 us (5%)
    pallas_call x1, Pallas kernels, per_device(): pl.pallas_call(functools.partial(kernel, nz, ncol), out_shape=jax.ShapeDt...  133 us
    unnamed x11, local copies, waits for them, and re-layouts  6.46 us

profile of v1, /device:TPU:1, one launch (start us, length us, event | category | flops | bytes accessed | tf_op | source)
XLA Modules:
  0.0 139.4 jit_solution(11216255693446488368)
XLA Ops:
  0.0 0.0 copy-start
  0.0 1.6 %copy-done = bf16[1,1,1,1,1024,1024]{5,4,3,2,1,0:T(8,128)(2,1)S(1)} copy-done((bf16[1,1,1,1,1024,1024]{5,4,3,2,1,0:T(8,128)(2,1)S(1)}, bf16[1,1,1,1,1024,1024]{5,4,3,2,1,0:T(8,128)(2,1)}, u32[]{:S(2)}) %copy-start) | copy-done | bytes 2097176
  1.6 0.0 copy-start.1
  1.6 1.2 copy-done.1
  2.8 0.0 copy-start.2
  2.8 1.0 copy-done.2
  3.9 0.0 copy-start.3
  3.9 1.0 copy-done.3
  4.9 0.0 copy-start.4
  4.9 0.9 copy-done.4
  5.8 132.9 %shard_map.55 = f32[64,512]{1,0:T(8,128)S(1)} custom-call(f32[64,512]{1,0:T(8,128)S(1)} %bitcast.9, bf16[1024,1024]{1,0:T(8,128)(2,1)S(1)} %bitcast.5, bf16[1024,512]{1,0:T(8,128)(2,1)S(1)} %bitcast.6, bf16[4,64,1024]{2,1,0:T(8,128)(2,1)S(1)} %bitcast.7, bf16[4,64,1024]{2,1,0:T(8,128)(2,1)S(1)} %copy-done.3), custom_call_target="tpu_custom_call" | custom-call | tf_op jit(solution)/shard_map/pallas_call | solution.py:378
  138.7 0.7 copy.7
Async XLA Ops:
  0.0 1.6 %copy-start = (bf16[1,1,1,1,1024,1024]{5,4,3,2,1,0:T(8,128)(2,1)S(1)}, bf16[1,1,1,1,1024,1024]{5,4,3,2,1,0:T(8,128)(2,1)}, u32[]{:S(2)}) copy-start(bf16[1,1,1,1,1024,1024]{5,4,3,2,1,0:T(8,128)(2,1)} %param.6) | copy-start | bytes 6291460
  1.6 1.2 copy-start.1
  2.8 1.0 copy-start.2
  3.9 1.0 copy-start.3
  4.9 0.9 copy-start.4

commit v2 on v1

--- a/solution.py
+++ b/solution.py
@@ -89,8 +89,14 @@
     for load in loads:
         load.start()
 
-    def on_col(d):
-        return (row, lax.rem(col + d, ncol))
+    near = ncol // 2
+    far = sorted(
+        ((dx, dy) for dx in range(2) for dy in range(near) if dx or dy),
+        key=lambda p: -(2 * p[0] + min(p[1], near - p[1])),
+    )
+
+    def on_col(dx, dy):
+        return (row, lax.rem(col // near + dx, 2) * near + lax.rem(col + dy, near))
 
     def on_z(d):
         return (lax.rem(zed + d, nz) * LEVEL + cls, col)
@@ -122,7 +128,10 @@
 
         return body
 
-    lax.fori_loop(1, ncol, greet(on_col), 0)
+    for dx, dy in far:
+        pl.semaphore_signal(
+            barrier, inc=1, device_id=on_col(dx, dy), device_id_type=MESH
+        )
     lax.fori_loop(1, nz, greet(on_z), 0)
     lax.fori_loop(1, LEVEL, greet(on_level), 0)
     pl.semaphore_wait(barrier, (ncol - 1) + (nz - 1) + (LEVEL - 1))
@@ -144,6 +153,33 @@
             relay(j, on_z(1)).start()
             if nz > 2:
                 relay(j, on_z(nz - 1)).start()
+
+    @pl.when(zed == 0)
+    def _():
+        picks = (
+            lax.broadcasted_iota(jnp.int32, (rows, size), 1)
+            == lax.broadcasted_iota(jnp.int32, (rows, size), 0) + col * rows
+        )
+        for k in range(ticks):
+            wsrc[k] = jnp.where(picks & (cls == k), 1.0, 0.0).astype(BF16)
+
+    @pl.when(zed > 0)
+    def _():
+        wsrc[...] = win[...]
+
+
+    beyond = lax.rem(cls + 2, LEVEL)
+    twin = cls + 1 - 2 * lax.rem(cls, 2)
+    on_beyond = (zed * LEVEL + beyond, col)
+    on_twin = (zed * LEVEL + twin, col)
+    remote(wsrc, wl.at[:, cls], wl_send, wl_recv.at[0], on_beyond).start()
+    remote(wsrc, wl.at[:, cls], wl_send, wl_recv.at[1], on_twin).start()
+    wl[:, cls] = wsrc[...]
+
+    def pass_on():
+        there = wl.at[:, beyond]
+        wait_for(there, wl_recv.at[0])
+        remote(there, there, wl_send, wl_recv.at[2], on_twin).start()
 
     loads[0].wait()
     loads[1].wait()
@@ -199,26 +235,6 @@
                 return carry
 
             lax.fori_loop(1, LEVEL, share, 0)
-
-    @pl.when(zed == 0)
-    def _():
-        picks = (
-            lax.broadcasted_iota(jnp.int32, (rows, size), 1)
-            == lax.broadcasted_iota(jnp.int32, (rows, size), 0) + col * rows
-        )
-        for k in range(ticks):
-            wsrc[k] = jnp.where(picks & (cls == k), 1.0, 0.0).astype(BF16)
-
-    @pl.when(zed > 0)
-    def _():
-        wsrc[...] = win[...]
-
-    def spread(d, carry):
-        remote(wsrc, wl.at[:, cls], wl_send, wl_recv, on_level(d)).start()
-        return carry
-
-    lax.fori_loop(1, LEVEL, spread, 0)
-    wl[:, cls] = wsrc[...]
 
     loads[4].wait()
     loads[3].wait()
@@ -270,11 +286,10 @@
     def gather(buf, k, value, send, recv):
         buf[k, col] = jnp.where(kept, value, 0.0).astype(BF16)
 
-        def body(d, carry):
-            remote(buf.at[k, col], buf.at[k, col], send.at[k], recv.at[k], on_col(d)).start()
-            return carry
-
-        lax.fori_loop(1, ncol, body, 0)
+        for dx, dy in far:
+            remote(
+                buf.at[k, col], buf.at[k, col], send.at[k], recv.at[k], on_col(dx, dy)
+            ).start()
 
     def whole(buf, k, recv):
         wait_for(buf.at[k, pl.ds(0, ncol - 1)], recv.at[k])
@@ -291,7 +306,8 @@
 
     def final(k):
         if k == 0:
-            wait_for(wl.at[:, pl.ds(0, LEVEL - 1)], wl_recv)
+            for way in range(1, 3):
+                wait_for(wsrc, wl_recv.at[way])
         if nz > 1:
             wait_for(sz.at[k, pl.ds(0, (nz - 1) * width)], z_recv.at[k])
         part = nt_dot(wl[k].reshape(LEVEL * rows, size), sz[k])
@@ -300,27 +316,33 @@
             usum[q] = piece if k == 0 else usum[q] + piece
 
     place = pl.multiple_of(zed * width, width)
+    def along(k):
+        part = sz.at[k, pl.ds(place, width), :]
+
+        def body(d, carry):
+            remote(part, part, z_send, z_recv.at[k], on_z(d)).start()
+            return carry
+
+        lax.fori_loop(1, nz, body, 0)
+
     solved = None
     for k in range(ticks):
         gather(a1, k, acc[k], a1_send, a1_recv)
         if k > 0:
+            along(k - 1)
             for later in range(k + 1, ticks):
                 update_row(k - 1, later, solved)
+        if k == 1:
+            pass_on()
         waiting = whole(a1, k, a1_recv)
         gather(a2, k, twice(nt_dot(waiting, dinv[k])), a2_send, a2_recv)
         if k >= 2:
             final(k - 2)
         solved = whole(a2, k, a2_recv)
         sz[k, pl.ds(place, width), :] = solved
-
-        def along(d, carry):
-            part = sz.at[k, pl.ds(place, width), :]
-            remote(part, part, z_send, z_recv.at[k], on_z(d)).start()
-            return carry
-
-        lax.fori_loop(1, nz, along, 0)
         if k + 1 < ticks:
             update_row(k, k + 1, solved)
+    along(ticks - 1)
 
     for k in range(max(ticks - 2, 0), ticks):
         final(k)
@@ -341,7 +363,8 @@
     wait_for(recv1, rs_send)
     wait_for(ub.at[pl.ds(0, LEVEL - 1)], u_send)
     wait_for(pin.at[pl.ds(0, LEVEL - 1)], sb_send)
-    wait_for(wl.at[:, pl.ds(0, LEVEL - 1)], wl_send)
+    for _ in range(3):
+        wait_for(wsrc, wl_send)
     for k in range(ticks):
         wait_for(a1.at[k, pl.ds(0, ncol - 1)], a1_send.at[k])
         wait_for(a2.at[k, pl.ds(0, ncol - 1)], a2_send.at[k])
@@ -413,7 +436,7 @@
             dma,
             dma((LEVEL - 1, LEVEL - 1)),
             dma,
-            dma,
+            dma((3,)),
             dma((ticks,)),
             dma((ticks,)),
             dma((ticks,)),
@@ -426,7 +449,7 @@
         compiler_params=pltpu.CompilerParams(
             collective_id=0,
             has_side_effects=True,
-            vmem_limit_bytes=40 * 1024 * 1024,
+            vmem_limit_bytes=60 * 1024 * 1024,
         ),
     )(
         right_side.reshape(rows, columns),

time: 140 us -> 115 us (0.82)
  Pallas kernels: 133 us -> 113 us
  local copies, waits for them, and re-layouts: 6.46 us -> 1.57 us
    pallas_call x1, Pallas kernels: 133 us -> 113 us  [per_device(): pl.pallas_call(functools.partial(kernel, nz, ncol), out_shape=jax.ShapeDt...]
    unnamed x11 -> x1, local copies, waits for them, and re-layouts: 6.46 us -> 1.57 us
where the time goes in v2:
time: 115 us; the launch traced here: 114 us
  Pallas kernels  113 us (98%)
  local copies, waits for them, and re-layouts  1.57 us (1%)
    pallas_call x1, Pallas kernels, per_device(): pl.pallas_call(functools.partial(kernel, nz, ncol), out_shape=jax.ShapeDt...  113 us

profile of v2, /device:TPU:1, one launch (start us, length us, event | category | flops | bytes accessed | tf_op | source)
XLA Modules:
  0.0 114.2 jit_solution(12080347873198110558)
XLA Ops:
  0.0 112.6 %shard_map.55 = f32[64,512]{1,0:T(8,128)} custom-call(f32[64,512]{1,0:T(8,128)} %bitcast.9, bf16[1024,1024]{1,0:T(8,128)(2,1)} %bitcast.5, bf16[1024,512]{1,0:T(8,128)(2,1)} %bitcast.6, bf16[4,64,1024]{2,1,0:T(8,128)(2,1)} %bitcast.7, bf16[4,64,1024]{2,1,0:T(8,128)(2,1)} %dinv_h.1), custom_call_target="tpu_custom_call" | custom-call | tf_op jit(solution)/shard_map/pallas_call | solution.py:401
  112.6 1.6 %copy.7 = f32[1,1,64,512]{3,2,1,0:T(8,128)} copy(f32[1,1,64,512]{3,2,1,0:T(8,128)} %bitcast.8) | data formatting | bytes 262144

commit v3 on v2

v3 whole, which is shorter than its diff:
```python
import functools

import jax
import jax.numpy as jnp
from jax import lax
from jax.experimental import pallas as pl
from jax.experimental.pallas import tpu as pltpu
from jax.sharding import PartitionSpec as P

MESH = pl.DeviceIdType.MESH
F32 = jnp.float32
BF16 = jnp.bfloat16
LEVEL = 4
LANES = 128


def nt_dot(a, b):
    return lax.dot_general(
        a, b, (((1,), (1,)), ((), ())), preferred_element_type=F32
    )


def kernel(
    nz,
    ncol,
    rhs_h,
    panel_h,
    prior_h,
    win_h,
    dinv_h,
    out_ref,
    rhs,
    panel,
    prior,
    win,
    dinv,
    sendx,
    sendy,
    own,
    recvx,
    recvy,
    pend,
    pt,
    sca,
    pin,
    acc,
    turn,
    sz,
    wsrc,
    wl,
    wc,
    ybuf,
    tt,
    usum,
    ub,
    load_sem,
    x_send,
    x_recv,
    rs_send,
    rs_recv,
    sa_send,
    sa_recv,
    sb_send,
    sb_recv,
    wr_send,
    wr_recv,
    wc_send,
    wc_recv,
    wl_send,
    wl_recv,
    y_send,
    y_recv,
    tz_send,
    tz_recv,
    ts_send,
    ts_recv,
    t_send,
    t_recv,
    z_send,
    z_recv,
    u_send,
    u_recv,
):
    row = lax.axis_index("row")
    col = lax.axis_index("col")
    zed = row // LEVEL
    cls = row % LEVEL
    ticks, rows, size = win.shape
    width = pin.shape[1]
    columns = rhs.shape[1]
    near = ncol // 2
    half_at = col // near
    lane_at = col % near
    parity = col % 2

    loads = [
        pltpu.make_async_copy(src, dst, load_sem.at[i])
        for i, (src, dst) in enumerate(
            ((prior_h, prior), (panel_h, panel), (dinv_h, dinv), (win_h, win), (rhs_h, rhs))
        )
    ]
    for load in loads:
        load.start()

    far = sorted(
        ((dx, dy) for dx in range(2) for dy in range(near) if dx or dy),
        key=lambda p: -(2 * p[0] + min(p[1], near - p[1])),
    )

    def on_col(dx, dy):
        return (row, lax.rem(half_at + dx, 2) * near + lax.rem(lane_at + dy, near))

    def on_z(d):
        return (lax.rem(zed + d, nz) * LEVEL + cls, col)

    along_z = sorted(range(1, nz), key=lambda d: -min(d, nz - d))

    def on_level(d):
        return (zed * LEVEL + lax.rem(cls + d, LEVEL), col)

    def remote(src, dst, send, recv, device):
        return pltpu.make_async_remote_copy(
            src_ref=src,
            dst_ref=dst,
            send_sem=send,
            recv_sem=recv,
            device_id=device,
            device_id_type=MESH,
        )

    def wait_for(ref, sem):
        pltpu.make_async_copy(ref, ref, sem).wait()

    barrier = pltpu.get_barrier_semaphore()
    friends = [on_col(dx, dy) for dx, dy in far]
    friends += [on_z(d) for d in range(1, nz)] + [on_level(d) for d in range(1, LEVEL)]
    for friend in friends:
        pl.semaphore_signal(barrier, inc=1, device_id=friend, device_id_type=MESH)

    loads[0].wait()
    loads[1].wait()
    per_block = min(4, near)

    def product(at, out):
        def body(i, carry):
            start = pl.multiple_of((at * near + i * per_block) * rows, per_block * rows)
            part = jnp.dot(
                panel[pl.ds(start, per_block * rows), :],
                prior[...],
                preferred_element_type=F32,
            ).astype(out.dtype)
            for t in range(per_block):
                out[i * per_block + t] = part[t * rows : (t + 1) * rows]
            return carry

        lax.fori_loop(0, near // per_block, body, 0)

    order = sorted(range(near), key=lambda d: -min(d, near - d))
    product(1 - half_at, sendx)
    pl.semaphore_wait(barrier, len(friends))
    for i, dy in enumerate(order):
        to = lax.rem(lane_at + dy, near)
        remote(sendx.at[to], recvx.at[to], x_send, x_recv.at[i], on_col(1, 0)).start()

    loads[2].wait()
    loads[3].wait()
    active = cls >= 1
    mine = jnp.maximum(cls - 1, 0)

    def set_out(j):
        wc[mine, j] = win[j]
        for d in along_z:
            block = wc.at[mine, j]
            remote(block, block, wr_send, wr_recv.at[j], on_z(d)).start()

    @pl.when(active & (zed == 0))
    def _():
        set_out(mine)

    group = nz - 1 - zed
    lowest = group * (size // nz) // rows
    tile = pl.ds(pl.multiple_of(group * LANES, LANES), LANES)

    @pl.when(active & (col >= lowest))
    def _():
        ybuf[col] = dinv[mine, :, tile]
        for dx, dy in far:
            remote(
                ybuf.at[col], ybuf.at[col], y_send, y_recv.at[col], on_col(dx, dy)
            ).start()

    product(half_at, own)

    @pl.when(active)
    def _():
        @pl.when(zed > 0)
        def _():
            wait_for(wc.at[mine, mine], wr_recv.at[mine])

        for c in range(ncol):

            @pl.when((c >= lowest) & (col != c))
            def _():
                wait_for(ybuf.at[c], y_recv.at[c])

            @pl.when(c < lowest)
            def _():
                ybuf[c] = jnp.zeros((rows, LANES), BF16)

        tt[mine, group] = jnp.dot(
            wc[mine, mine], ybuf[...].reshape(size, LANES), preferred_element_type=F32
        ).astype(BF16)
        for d in along_z:
            part = tt.at[mine, group]
            remote(part, part, tz_send, tz_recv, on_z(d)).start()

    for i, dy in enumerate(order):
        to = lax.rem(lane_at + dy, near)
        wait_for(recvx.at[to], x_recv.at[i])
        both = own[to] + recvx[to].astype(F32)
        if dy == 0:
            own[to] = both
        else:
            sendy[to] = both.astype(BF16)
            remote(
                sendy.at[to], recvy.at[dy - 1], rs_send, rs_recv, on_col(0, dy)
            ).start()

    beyond = lax.rem(cls + 2, LEVEL)
    twin = cls + 1 - 2 * lax.rem(cls, 2)
    on_beyond = (zed * LEVEL + beyond, col)
    on_twin = (zed * LEVEL + twin, col)

    def exchange():
        @pl.when(zed == 0)
        def _():
            picks = (
                lax.broadcasted_iota(jnp.int32, (rows, size), 1)
                == lax.broadcasted_iota(jnp.int32, (rows, size), 0) + col * rows
            )
            for k in range(ticks):
                wsrc[k] = jnp.where(picks & (cls == k), 1.0, 0.0).astype(BF16)

        @pl.when(zed > 0)
        def _():
            wsrc[...] = win[...]

        remote(wsrc, wl.at[:, cls], wl_send, wl_recv.at[0], on_beyond).start()
        remote(wsrc, wl.at[:, cls], wl_send, wl_recv.at[1], on_twin).start()
        wl[:, cls] = wsrc[...]

    def pass_on():
        there = wl.at[:, beyond]
        wait_for(there, wl_recv.at[0])
        remote(there, there, wl_send, wl_recv.at[2], on_twin).start()

    exchange()

    def settle():
        wait_for(recvy, rs_recv)
        total = own[lane_at]
        for d in range(near - 1):
            total = total + recvy[d].astype(F32)
        pend[...] = rhs[...] - total

    loads[4].wait()

    @pl.when(zed == 0)
    def _():
        settle()
        value = pend[...]
        for q in range(LEVEL):
            part = jnp.concatenate(
                [value[:, q * LANES : (q + 1) * LANES]] * 2, axis=0
            ).T.astype(BF16)
            for t in range(nz):
                pt[q, t] = part[t * width : (t + 1) * width]
        for d in along_z:
            remote(pt.at[:, d], sca, sa_send, sa_recv, on_z(d)).start()
        sca[...] = pt[:, 0]

    for j in range(LEVEL - 2):

        @pl.when((j < cls - 1) & (zed == 0))
        def _():
            set_out(j)

    def share_window():
        for j in range(LEVEL - 2):

            @pl.when(j < cls - 1)
            def _():
                block = wc.at[mine, j]

                @pl.when(zed > 0)
                def _():
                    wait_for(block, wr_recv.at[j])

                for d in range(1, LEVEL):
                    remote(
                        block, block, wc_send, wc_recv.at[mine, j], on_level(d)
                    ).start()

    @pl.when(zed > 0)
    def _():
        wait_for(sca, sa_recv)

    for d in range(1, LEVEL):
        to = lax.rem(cls + d, LEVEL)
        remote(sca.at[to], pin.at[cls], sb_send, sb_recv, on_level(d)).start()
    pin[cls] = sca[cls]

    @pl.when(active)
    def _():
        wait_for(tt.at[mine, pl.ds(0, nz - 1)], tz_recv)
        for d in range(1, LEVEL):
            part = tt.at[mine]
            remote(part, part, ts_send, ts_recv.at[mine], on_level(d)).start()

    wait_for(pin.at[pl.ds(0, LEVEL - 1)], sb_recv)
    for k in range(ticks):
        acc[k] = pin[k].astype(F32)

    lane = lax.broadcasted_iota(jnp.int32, (width, LANES), 1)
    kept = (lane >= parity * rows) & (lane < parity * rows + rows)

    def twice(value):
        return jnp.concatenate([value, value], axis=1)

    def put(n, slot, value):
        turn[n, col, slot] = jnp.where(kept, value, 0.0).astype(BF16)

    def slots(n):
        return pl.ds(0 if n < ticks else 1, 2 if 0 < n < ticks else 1)

    def gather(n):
        part = turn.at[n, col, slots(n)]
        for dx, dy in far:
            remote(part, part, t_send.at[n], t_recv.at[n], on_col(dx, dy)).start()

    def whole(n, slot):
        return jnp.concatenate(
            [turn[n, 2 * p, slot] + turn[n, 2 * p + 1, slot] for p in range(near)],
            axis=1,
        )

    def window_term(later, k, solved):
        @pl.when(cls != later)
        def _():
            wait_for(wc.at[later - 1, k], wc_recv.at[later - 1, k])

        return twice(nt_dot(solved, wc[later - 1, k]))

    def fold_term(n, waiting):
        @pl.when(cls != n + 1)
        def _():
            wait_for(tt.at[n], ts_recv.at[n])

        fold = jnp.concatenate([tt[n, g] for g in range(nz)], axis=1)
        return twice(nt_dot(waiting, fold))

    place = pl.multiple_of(zed * width, width)

    def along(k):
        part = sz.at[k, pl.ds(place, width), :]
        for d in along_z:
            remote(part, part, z_send, z_recv.at[k], on_z(d)).start()

    def final(k):
        if k == 0:
            for way in range(1, 3):
                wait_for(wsrc, wl_recv.at[way])
        wait_for(sz.at[k, pl.ds(0, (nz - 1) * width)], z_recv.at[k])
        part = nt_dot(wl[k].reshape(LEVEL * rows, size), sz[k])
        for q in range(LEVEL):
            piece = part[q * rows : (q + 1) * rows]
            usum[q] = piece if k == 0 else usum[q] + piece

    put(0, 0, acc[0])
    gather(0)
    for n in range(ticks + 1):
        wait_for(turn.at[n, pl.ds(0, ncol - 1), slots(n)], t_recv.at[n])
        solved = whole(n, 1) if n > 0 else None
        if n < ticks:
            waiting = whole(n, 0)
            put(n + 1, 1, twice(nt_dot(waiting, dinv[n])))
            if n + 1 < ticks:
                value = acc[n + 1] - fold_term(n, waiting)
                if n > 0:
                    value = value - window_term(n + 1, n - 1, solved)
                put(n + 1, 0, value)
            gather(n + 1)
        if n > 0:
            sz[n - 1, pl.ds(place, width), :] = solved
            along(n - 1)
            for later in range(n + 2, ticks):
                acc[later] = acc[later] - window_term(later, n - 1, solved)
        if n == 0:
            share_window()
        if n == 1:
            pass_on()

            @pl.when(zed > 0)
            def _():
                settle()

        if n >= 2:
            final(n - 2)
    final(ticks - 1)

    for d in range(1, LEVEL):
        to = lax.rem(cls + d, LEVEL)
        remote(usum.at[to], ub.at[cls], u_send, u_recv, on_level(d)).start()
    ub[cls] = usum[cls]
    wait_for(ub.at[pl.ds(0, LEVEL - 1)], u_recv)
    for q in range(LEVEL):
        cut = slice(q * LANES, (q + 1) * LANES)
        out_ref[:, cut] = jnp.where(zed == 0, ub[q], pend[:, cut] - ub[q])

    wait_for(recvx, x_send)
    wait_for(recvy, rs_send)
    wait_for(ub.at[pl.ds(0, LEVEL - 1)], u_send)
    wait_for(pin.at[pl.ds(0, LEVEL - 1)], sb_send)
    for _ in range(3):
        wait_for(wsrc, wl_send)
    for n in range(ticks + 1):
        wait_for(turn.at[n, pl.ds(0, ncol - 1), slots(n)], t_send.at[n])
    for k in range(ticks):
        wait_for(sz.at[k, pl.ds(0, (nz - 1) * width)], z_send)

    @pl.when(zed == 0)
    def _():
        wait_for(pt.at[:, pl.ds(0, nz - 1)], sa_send)

    @pl.when(active & (col >= lowest))
    def _():
        wait_for(ybuf.at[pl.ds(0, ncol - 1)], y_send)

    @pl.when(active)
    def _():
        wait_for(tt.at[mine, pl.ds(0, nz - 1)], tz_send)
        for _ in range(LEVEL - 1):
            wait_for(tt.at[mine], ts_send)

    for j in range(LEVEL - 1):

        @pl.when((j < cls) & (zed == 0))
        def _():
            for _ in along_z:
                wait_for(wc.at[mine, j], wr_send)

        @pl.when(j < cls - 1)
        def _():
            wait_for(wc.at[pl.ds(0, LEVEL - 1), j], wc_send)


def per_device(right_side, prior_panel, prior_solved, window_panel, diag_inverse):
    rows, columns = right_side.shape[2:]
    size = prior_panel.shape[4]
    ticks = window_panel.shape[2]
    ncol = lax.axis_size("col")
    nz = lax.axis_size("row") // LEVEL
    width = LANES // nz
    near = ncol // 2
    dma = pltpu.SemaphoreType.DMA
    vmem = pltpu.VMEM
    out = pl.pallas_call(
        functools.partial(kernel, nz, ncol),
        out_shape=jax.ShapeDtypeStruct((rows, columns), F32),
        in_specs=[pl.BlockSpec(memory_space=pl.ANY)] * 5,
        out_specs=pl.BlockSpec(memory_space=pltpu.VMEM),
        scratch_shapes=[
            vmem((rows, columns), F32),
            vmem((size, size), BF16),
            vmem((size, columns), BF16),
            vmem((ticks, rows, size), BF16),
            vmem((ticks, rows, size), BF16),
            vmem((near, rows, columns), BF16),
            vmem((near, rows, columns), BF16),
            vmem((near, rows, columns), F32),
            vmem((near, rows, columns), BF16),
            vmem((near - 1, rows, columns), BF16),
            vmem((rows, columns), F32),
            vmem((LEVEL, nz, width, LANES), BF16),
            vmem((LEVEL, width, LANES), BF16),
            vmem((LEVEL, width, LANES), BF16),
            vmem((ticks, width, LANES), F32),
            vmem((ticks + 1, ncol, 2, width, LANES), BF16),
            vmem((ticks, LANES, size), BF16),
            vmem((ticks, rows, size), BF16),
            vmem((ticks, LEVEL, rows, size), BF16),
            vmem((LEVEL - 1, LEVEL - 1, rows, size), BF16),
            vmem((ncol, rows, LANES), BF16),
            vmem((LEVEL - 1, nz, rows, LANES), BF16),
            vmem((LEVEL, rows, LANES), F32),
            vmem((LEVEL, rows, LANES), F32),
            dma((5,)),
            dma,
            dma((near,)),
            dma,
            dma,
            dma,
            dma,
            dma,
            dma,
            dma,
            dma((LEVEL - 1,)),
            dma,
            dma((LEVEL - 1, LEVEL - 1)),
            dma,
            dma((3,)),
            dma,
            dma((ncol,)),
            dma,
            dma,
            dma,
            dma((LEVEL - 1,)),
            dma((ticks + 1,)),
            dma((ticks + 1,)),
            dma,
            dma((ticks,)),
            dma,
            dma,
        ],
        compiler_params=pltpu.CompilerParams(
            collective_id=0,
            has_side_effects=True,
            vmem_limit_bytes=60 * 1024 * 1024,
        ),
    )(
        right_side.reshape(rows, columns),
        prior_panel.reshape(size, size),
        prior_solved.reshape(size, columns),
        window_panel.reshape(ticks, rows, size),
        diag_inverse,
    )
    return out.reshape(right_side.shape)


def solution(mesh):
    return jax.shard_map(
        per_device,
        mesh=mesh,
        in_specs=(
            P(None, "row", "col", None),
            P(None, "row", None, "col", None, None),
            P(None, "col", None, None),
            P(None, "row", None, "col", None),
            P(None, "col", None),
        ),
        out_specs=P(None, "row", "col", None),
        check_vma=False,
    )
```

time: 115 us -> 92.8 us (0.81)
  Pallas kernels: 113 us -> 90.6 us
    pallas_call x1, Pallas kernels: 113 us -> 90.6 us  [per_device(): pl.pallas_call(functools.partial(kernel, nz, ncol), out_shape=jax.ShapeDt...]
where the time goes in v3:
time: 92.8 us; the launch traced here: 92.2 us
  Pallas kernels  90.6 us (98%)
  local copies, waits for them, and re-layouts  1.57 us (2%)
    pallas_call x1, Pallas kernels, per_device(): pl.pallas_call(functools.partial(kernel, nz, ncol), out_shape=jax.ShapeDt...  90.6 us

profile of v3, /device:TPU:1, one launch (start us, length us, event | category | flops | bytes accessed | tf_op | source)
XLA Modules:
  0.0 92.2 jit_solution(13098234431440704579)
XLA Ops:
  0.0 90.6 %shard_map.55 = f32[64,512]{1,0:T(8,128)} custom-call(f32[64,512]{1,0:T(8,128)} %bitcast.9, bf16[1024,1024]{1,0:T(8,128)(2,1)} %bitcast.5, bf16[1024,512]{1,0:T(8,128)(2,1)} %bitcast.6, bf16[4,64,1024]{2,1,0:T(8,128)(2,1)} %bitcast.7, bf16[4,64,1024]{2,1,0:T(8,128)(2,1)} %dinv_h.1), custom_call_target="tpu_custom_call" | custom-call | tf_op jit(solution)/shard_map/pallas_call | solution.py:467
  90.6 1.6 %copy.7 = f32[1,1,64,512]{3,2,1,0:T(8,128)} copy(f32[1,1,64,512]{3,2,1,0:T(8,128)} %bitcast.8) | data formatting | bytes 262144

commit v4 on v3

--- a/solution.py
+++ b/solution.py
@@ -46,7 +46,6 @@
     acc,
     turn,
     sz,
-    wsrc,
     wl,
     wc,
     ybuf,
@@ -64,6 +63,10 @@
     sb_recv,
     wr_send,
     wr_recv,
+    wh_send,
+    wh_recv,
+    wo_send,
+    wo_recv,
     wc_send,
     wc_recv,
     wl_send,
@@ -157,29 +160,28 @@
 
     order = sorted(range(near), key=lambda d: -min(d, near - d))
     product(1 - half_at, sendx)
-    pl.semaphore_wait(barrier, len(friends))
-    for i, dy in enumerate(order):
-        to = lax.rem(lane_at + dy, near)
-        remote(sendx.at[to], recvx.at[to], x_send, x_recv.at[i], on_col(1, 0)).start()
-
     loads[2].wait()
     loads[3].wait()
     active = cls >= 1
     mine = jnp.maximum(cls - 1, 0)
-
-    def set_out(j):
-        wc[mine, j] = win[j]
-        for d in along_z:
-            block = wc.at[mine, j]
-            remote(block, block, wr_send, wr_recv.at[j], on_z(d)).start()
-
-    @pl.when(active & (zed == 0))
-    def _():
-        set_out(mine)
+    carrier = cls < LEVEL - 1
+    carried = wc.at[jnp.where(cls == 2, 1, 2), jnp.where(cls == 1, 1, 0)]
+    begin = near // 2
+    trunk = sorted(range(2, nz, 2), key=lambda d: -min(d, nz - d)) or [1]
+    branch = (zed % 4 == 2) if nz > 2 else (zed < 0)
+
+    def set_out(i, block, send, recv):
+        if i in range(len(trunk)):
+            remote(block, block, send, recv, on_z(trunk[i])).start()
+
+    def branch_out(block, send, recv):
+        for d in (1, nz - 1):
+            remote(block, block, send, recv, on_z(d)).start()
 
     group = nz - 1 - zed
     lowest = group * (size // nz) // rows
     tile = pl.ds(pl.multiple_of(group * LANES, LANES), LANES)
+    pl.semaphore_wait(barrier, len(friends))
 
     @pl.when(active & (col >= lowest))
     def _():
@@ -189,14 +191,48 @@
                 ybuf.at[col], ybuf.at[col], y_send, y_recv.at[col], on_col(dx, dy)
             ).start()
 
+    def send_x(some):
+        for i in some:
+            to = lax.rem(lane_at + order[i], near)
+            remote(sendx.at[to], recvx.at[to], x_send, x_recv.at[i], on_col(1, 0)).start()
+
+    def first_out(who):
+        @pl.when((zed == 0) & who)
+        def _():
+            wc[mine, mine] = win[mine]
+            for i in range(len(trunk)):
+                set_out(i, wc.at[mine, mine], wr_send, wr_recv)
+
+    first_out(cls == 1)
+    send_x(range(begin))
+
+    @pl.when(zed == 0)
+    def _():
+        send_x(range(begin, near))
+
+    first_out(cls > 1)
+
+    @pl.when((zed == 0) & (cls == LEVEL - 1))
+    def _():
+        for j in range(2):
+            remote(win.at[j], wc.at[2, j], wh_send, wh_recv, (j, col)).start()
+
     product(half_at, own)
 
+    @pl.when(active & (zed > 0))
+    def _():
+        wait_for(wc.at[mine, mine], wr_recv)
+
+        @pl.when(branch)
+        def _():
+            branch_out(wc.at[mine, mine], wr_send, wr_recv)
+
+    @pl.when(zed > 0)
+    def _():
+        send_x(range(begin, near))
+
     @pl.when(active)
     def _():
-        @pl.when(zed > 0)
-        def _():
-            wait_for(wc.at[mine, mine], wr_recv.at[mine])
-
         for c in range(ncol):
 
             @pl.when((c >= lowest) & (col != c))
@@ -213,6 +249,12 @@
         for d in along_z:
             part = tt.at[mine, group]
             remote(part, part, tz_send, tz_recv, on_z(d)).start()
+
+    beyond = lax.rem(cls + 2, LEVEL)
+    twin = cls + 1 - 2 * lax.rem(cls, 2)
+    on_beyond = (zed * LEVEL + beyond, col)
+    on_twin = (zed * LEVEL + twin, col)
+    pieces = 2 * ticks // near
 
     for i, dy in enumerate(order):
         to = lax.rem(lane_at + dy, near)
@@ -226,12 +268,33 @@
                 sendy.at[to], recvy.at[dy - 1], rs_send, rs_recv, on_col(0, dy)
             ).start()
 
-    beyond = lax.rem(cls + 2, LEVEL)
-    twin = cls + 1 - 2 * lax.rem(cls, 2)
-    on_beyond = (zed * LEVEL + beyond, col)
-    on_twin = (zed * LEVEL + twin, col)
-
-    def exchange():
+        @pl.when(zed > 0)
+        def _():
+            for piece in range(i * pieces, (i + 1) * pieces):
+                k, side = piece // 2, pl.ds(piece % 2 * (rows // 2), rows // 2)
+                remote(
+                    win.at[k, side], wl.at[k, cls, side], wl_send, wl_recv.at[0], on_beyond
+                ).start()
+
+        if i == begin - 1:
+
+            @pl.when((zed == 0) & (cls == 2))
+            def _():
+                wc[1, 0] = win[0]
+
+            @pl.when((zed == 0) & (cls < 2))
+            def _():
+                wait_for(carried, wh_recv)
+
+        @pl.when((zed == 0) & carrier)
+        def _():
+            set_out(i + 1 - begin, carried, wo_send, wo_recv)
+
+    @pl.when(zed > 0)
+    def _():
+        remote(win, wl.at[:, cls], wl_send, wl_recv.at[1], on_twin).start()
+
+    def pass_on():
         @pl.when(zed == 0)
         def _():
             picks = (
@@ -239,22 +302,15 @@
                 == lax.broadcasted_iota(jnp.int32, (rows, size), 0) + col * rows
             )
             for k in range(ticks):
-                wsrc[k] = jnp.where(picks & (cls == k), 1.0, 0.0).astype(BF16)
+                for q in range(LEVEL):
+                    wl[k, q] = jnp.where(picks & (k == q), 1.0, 0.0).astype(BF16)
 
         @pl.when(zed > 0)
         def _():
-            wsrc[...] = win[...]
-
-        remote(wsrc, wl.at[:, cls], wl_send, wl_recv.at[0], on_beyond).start()
-        remote(wsrc, wl.at[:, cls], wl_send, wl_recv.at[1], on_twin).start()
-        wl[:, cls] = wsrc[...]
-
-    def pass_on():
-        there = wl.at[:, beyond]
-        wait_for(there, wl_recv.at[0])
-        remote(there, there, wl_send, wl_recv.at[2], on_twin).start()
-
-    exchange()
+            wl[:, cls] = win[...]
+            there = wl.at[:, beyond]
+            wait_for(there, wl_recv.at[0])
+            remote(there, there, wl_send, wl_recv.at[2], on_twin).start()
 
     def settle():
         wait_for(recvy, rs_recv)
@@ -279,47 +335,33 @@
             remote(pt.at[:, d], sca, sa_send, sa_recv, on_z(d)).start()
         sca[...] = pt[:, 0]
 
-    for j in range(LEVEL - 2):
-
-        @pl.when((j < cls - 1) & (zed == 0))
-        def _():
-            set_out(j)
-
-    def share_window():
-        for j in range(LEVEL - 2):
-
-            @pl.when(j < cls - 1)
-            def _():
-                block = wc.at[mine, j]
-
-                @pl.when(zed > 0)
-                def _():
-                    wait_for(block, wr_recv.at[j])
-
-                for d in range(1, LEVEL):
-                    remote(
-                        block, block, wc_send, wc_recv.at[mine, j], on_level(d)
-                    ).start()
-
-    @pl.when(zed > 0)
-    def _():
-        wait_for(sca, sa_recv)
-
-    for d in range(1, LEVEL):
-        to = lax.rem(cls + d, LEVEL)
-        remote(sca.at[to], pin.at[cls], sb_send, sb_recv, on_level(d)).start()
-    pin[cls] = sca[cls]
-
-    @pl.when(active)
-    def _():
-        wait_for(tt.at[mine, pl.ds(0, nz - 1)], tz_recv)
-        for d in range(1, LEVEL):
-            part = tt.at[mine]
-            remote(part, part, ts_send, ts_recv.at[mine], on_level(d)).start()
-
-    wait_for(pin.at[pl.ds(0, LEVEL - 1)], sb_recv)
-    for k in range(ticks):
-        acc[k] = pin[k].astype(F32)
+    @pl.when((zed > 0) & branch & carrier)
+    def _():
+        wait_for(carried, wo_recv)
+        branch_out(carried, wo_send, wo_recv)
+
+    def deal(who):
+        @pl.when(who & (zed > 0))
+        def _():
+            wait_for(sca, sa_recv)
+
+        @pl.when(who)
+        def _():
+            for d in range(1, LEVEL):
+                to = lax.rem(cls + d, LEVEL)
+                remote(
+                    sca.at[to], pin.at[cls], sb_send, sb_recv.at[cls], on_level(d)
+                ).start()
+            pin[cls] = sca[cls]
+
+    def take(k):
+        @pl.when(cls != k)
+        def _():
+            wait_for(pin.at[k], sb_recv.at[k])
+
+        return pin[k].astype(F32)
+
+    deal(cls == 0)
 
     lane = lax.broadcasted_iota(jnp.int32, (width, LANES), 1)
     kept = (lane >= parity * rows) & (lane < parity * rows + rows)
@@ -345,7 +387,7 @@
         )
 
     def window_term(later, k, solved):
-        @pl.when(cls != later)
+        @pl.when(cls != (2 if later == 2 else k))
         def _():
             wait_for(wc.at[later - 1, k], wc_recv.at[later - 1, k])
 
@@ -368,18 +410,47 @@
 
     def final(k):
         if k == 0:
-            for way in range(1, 3):
-                wait_for(wsrc, wl_recv.at[way])
+
+            @pl.when(zed > 0)
+            def _():
+                for way in range(1, 3):
+                    wait_for(win, wl_recv.at[way])
+
         wait_for(sz.at[k, pl.ds(0, (nz - 1) * width)], z_recv.at[k])
         part = nt_dot(wl[k].reshape(LEVEL * rows, size), sz[k])
         for q in range(LEVEL):
             piece = part[q * rows : (q + 1) * rows]
             usum[q] = piece if k == 0 else usum[q] + piece
 
-    put(0, 0, acc[0])
+    def share_fold(who):
+        @pl.when(who)
+        def _():
+            wait_for(tt.at[mine, pl.ds(0, nz - 1)], tz_recv)
+            for d in range(1, LEVEL):
+                part = tt.at[mine]
+                remote(part, part, ts_send, ts_recv.at[mine], on_level(d)).start()
+
+    def share_window(who):
+        @pl.when(who)
+        def _():
+            @pl.when((zed > 0) & jnp.logical_not(branch))
+            def _():
+                wait_for(carried, wo_recv)
+
+            at = jnp.where(cls == 2, 1, 2), jnp.where(cls == 1, 1, 0)
+            for d in range(1, LEVEL):
+                remote(carried, carried, wc_send, wc_recv.at[at], on_level(d)).start()
+
+    put(0, 0, take(0))
     gather(0)
+    deal(cls > 0)
+    share_fold((cls == 1) | (cls == 2))
+    share_window((cls == 0) | (cls == 2))
     for n in range(ticks + 1):
         wait_for(turn.at[n, pl.ds(0, ncol - 1), slots(n)], t_recv.at[n])
+        if n == 0:
+            for k in range(1, ticks):
+                acc[k] = take(k)
         solved = whole(n, 1) if n > 0 else None
         if n < ticks:
             waiting = whole(n, 0)
@@ -396,7 +467,8 @@
             for later in range(n + 2, ticks):
                 acc[later] = acc[later] - window_term(later, n - 1, solved)
         if n == 0:
-            share_window()
+            share_fold(cls == 3)
+            share_window(cls == 1)
         if n == 1:
             pass_on()
 
@@ -421,8 +493,12 @@
     wait_for(recvy, rs_send)
     wait_for(ub.at[pl.ds(0, LEVEL - 1)], u_send)
     wait_for(pin.at[pl.ds(0, LEVEL - 1)], sb_send)
-    for _ in range(3):
-        wait_for(wsrc, wl_send)
+
+    @pl.when(zed > 0)
+    def _():
+        for _ in range(3):
+            wait_for(win, wl_send)
+
     for n in range(ticks + 1):
         wait_for(turn.at[n, pl.ds(0, ncol - 1), slots(n)], t_send.at[n])
     for k in range(ticks):
@@ -442,16 +518,33 @@
         for _ in range(LEVEL - 1):
             wait_for(tt.at[mine], ts_send)
 
-    for j in range(LEVEL - 1):
-
-        @pl.when((j < cls) & (zed == 0))
-        def _():
-            for _ in along_z:
-                wait_for(wc.at[mine, j], wr_send)
-
-        @pl.when(j < cls - 1)
-        def _():
-            wait_for(wc.at[pl.ds(0, LEVEL - 1), j], wc_send)
+    @pl.when(active & (zed == 0))
+    def _():
+        for _ in trunk:
+            wait_for(wc.at[mine, mine], wr_send)
+
+    @pl.when(carrier & (zed == 0))
+    def _():
+        for _ in trunk:
+            wait_for(carried, wo_send)
+
+    @pl.when(active & branch)
+    def _():
+        for _ in range(2):
+            wait_for(wc.at[mine, mine], wr_send)
+
+    @pl.when(carrier & branch)
+    def _():
+        for _ in range(2):
+            wait_for(carried, wo_send)
+
+    @pl.when((zed == 0) & (cls == LEVEL - 1))
+    def _():
+        wait_for(wc.at[2, pl.ds(0, 2)], wh_send)
+
+    @pl.when(carrier)
+    def _():
+        wait_for(wc.at[0], wc_send)
 
 
 def per_device(right_side, prior_panel, prior_solved, window_panel, diag_inverse):
@@ -487,7 +580,6 @@
             vmem((ticks, width, LANES), F32),
             vmem((ticks + 1, ncol, 2, width, LANES), BF16),
             vmem((ticks, LANES, size), BF16),
-            vmem((ticks, rows, size), BF16),
             vmem((ticks, LEVEL, rows, size), BF16),
             vmem((LEVEL - 1, LEVEL - 1, rows, size), BF16),
             vmem((ncol, rows, LANES), BF16),
@@ -502,9 +594,13 @@
             dma,
             dma,
             dma,
-            dma,
-            dma,
-            dma((LEVEL - 1,)),
+            dma((LEVEL,)),
+            dma,
+            dma,
+            dma,
+            dma,
+            dma,
+            dma,
             dma,
             dma((LEVEL - 1, LEVEL - 1)),
             dma,

time: 92.8 us -> 88.2 us (0.950)
  Pallas kernels: 90.6 us -> 86.5 us
    pallas_call x1, Pallas kernels: 90.6 us -> 86.5 us  [per_device(): pl.pallas_call(functools.partial(kernel, nz, ncol), out_shape=jax.ShapeDt...]
where the time goes in v4:
time: 88.2 us; the launch traced here: 88 us
  Pallas kernels  86.5 us (98%)
  local copies, waits for them, and re-layouts  1.57 us (2%)
    pallas_call x1, Pallas kernels, per_device(): pl.pallas_call(functools.partial(kernel, nz, ncol), out_shape=jax.ShapeDt...  86.5 us

profile of v4, /device:TPU:1, one launch (start us, length us, event | category | flops | bytes accessed | tf_op | source)
XLA Modules:
  0.0 88.0 jit_solution(5545337271293211900)
XLA Ops:
  0.0 86.5 %shard_map.55 = f32[64,512]{1,0:T(8,128)} custom-call(f32[64,512]{1,0:T(8,128)} %bitcast.9, bf16[1024,1024]{1,0:T(8,128)(2,1)} %bitcast.5, bf16[1024,512]{1,0:T(8,128)(2,1)} %bitcast.6, bf16[4,64,1024]{2,1,0:T(8,128)(2,1)} %bitcast.7, bf16[4,64,1024]{2,1,0:T(8,128)(2,1)} %dinv_h.1), custom_call_target="tpu_custom_call" | custom-call | tf_op jit(solution)/shard_map/pallas_call | solution.py:560
  86.5 1.6 %copy.7 = f32[1,1,64,512]{3,2,1,0:T(8,128)} copy(f32[1,1,64,512]{3,2,1,0:T(8,128)} %bitcast.8) | data formatting | bytes 262144

commit v5 on v4

--- a/solution.py
+++ b/solution.py
@@ -135,9 +135,10 @@
         pltpu.make_async_copy(ref, ref, sem).wait()
 
     barrier = pltpu.get_barrier_semaphore()
-    friends = [on_col(dx, dy) for dx, dy in far]
-    friends += [on_z(d) for d in range(1, nz)] + [on_level(d) for d in range(1, LEVEL)]
-    for friend in friends:
+    friends = [(2 * dx + min(dy, near - dy), on_col(dx, dy)) for dx, dy in far]
+    friends += [(min(d, nz - d), on_z(d)) for d in along_z]
+    friends += [(1, on_level(d)) for d in range(1, LEVEL)]
+    for _, friend in sorted(friends, key=lambda p: -p[0]):
         pl.semaphore_signal(barrier, inc=1, device_id=friend, device_id_type=MESH)
 
     loads[0].wait()
@@ -254,7 +255,6 @@
     twin = cls + 1 - 2 * lax.rem(cls, 2)
     on_beyond = (zed * LEVEL + beyond, col)
     on_twin = (zed * LEVEL + twin, col)
-    pieces = 2 * ticks // near
 
     for i, dy in enumerate(order):
         to = lax.rem(lane_at + dy, near)
@@ -268,31 +268,16 @@
                 sendy.at[to], recvy.at[dy - 1], rs_send, rs_recv, on_col(0, dy)
             ).start()
 
+    def hand_over(some):
         @pl.when(zed > 0)
         def _():
-            for piece in range(i * pieces, (i + 1) * pieces):
+            for piece in some:
                 k, side = piece // 2, pl.ds(piece % 2 * (rows // 2), rows // 2)
                 remote(
                     win.at[k, side], wl.at[k, cls, side], wl_send, wl_recv.at[0], on_beyond
                 ).start()
 
-        if i == begin - 1:
-
-            @pl.when((zed == 0) & (cls == 2))
-            def _():
-                wc[1, 0] = win[0]
-
-            @pl.when((zed == 0) & (cls < 2))
-            def _():
-                wait_for(carried, wh_recv)
-
-        @pl.when((zed == 0) & carrier)
-        def _():
-            set_out(i + 1 - begin, carried, wo_send, wo_recv)
-
-    @pl.when(zed > 0)
-    def _():
-        remote(win, wl.at[:, cls], wl_send, wl_recv.at[1], on_twin).start()
+    hand_over(range(4))
 
     def pass_on():
         @pl.when(zed == 0)
@@ -335,11 +320,6 @@
             remote(pt.at[:, d], sca, sa_send, sa_recv, on_z(d)).start()
         sca[...] = pt[:, 0]
 
-    @pl.when((zed > 0) & branch & carrier)
-    def _():
-        wait_for(carried, wo_recv)
-        branch_out(carried, wo_send, wo_recv)
-
     def deal(who):
         @pl.when(who & (zed > 0))
         def _():
@@ -363,6 +343,19 @@
 
     deal(cls == 0)
 
+    @pl.when((zed == 0) & carrier)
+    def _():
+        @pl.when(cls == 2)
+        def _():
+            wc[1, 0] = win[0]
+
+        @pl.when(cls < 2)
+        def _():
+            wait_for(carried, wh_recv)
+
+        for i in range(len(trunk)):
+            set_out(i, carried, wo_send, wo_recv)
+
     lane = lax.broadcasted_iota(jnp.int32, (width, LANES), 1)
     kept = (lane >= parity * rows) & (lane < parity * rows + rows)
 
@@ -377,8 +370,9 @@
 
     def gather(n):
         part = turn.at[n, col, slots(n)]
+        arrived = t_recv.at[n + half_at if n == ticks else n]
         for dx, dy in far:
-            remote(part, part, t_send.at[n], t_recv.at[n], on_col(dx, dy)).start()
+            remote(part, part, t_send.at[n], arrived, on_col(dx, dy)).start()
 
     def whole(n, slot):
         return jnp.concatenate(
@@ -444,9 +438,41 @@
     put(0, 0, take(0))
     gather(0)
     deal(cls > 0)
+
+    @pl.when(branch & carrier)
+    def _():
+        wait_for(carried, wo_recv)
+        branch_out(carried, wo_send, wo_recv)
+
     share_fold((cls == 1) | (cls == 2))
-    share_window((cls == 0) | (cls == 2))
+    share_window(cls == 2)
+    def finish():
+        for step in range(2):
+            part_at = lax.rem(half_at + step, 2)
+            wait_for(
+                turn.at[ticks, pl.ds(0, near - 1 + step), slots(ticks)],
+                t_recv.at[ticks + part_at],
+            )
+            value = jnp.concatenate(
+                [
+                    turn[ticks, part_at * near + 2 * p, 1]
+                    + turn[ticks, part_at * near + 2 * p + 1, 1]
+                    for p in range(near // 2)
+                ],
+                axis=1,
+            )
+            lanes = pl.ds(pl.multiple_of(part_at * (size // 2), LANES), size // 2)
+            sz[ticks - 1, pl.ds(place, width), lanes] = value
+            part = sz.at[ticks - 1, pl.ds(place, width), lanes]
+            for d in along_z:
+                remote(part, part, z_send, z_recv.at[ticks - 1], on_z(d)).start()
+
     for n in range(ticks + 1):
+        if n == ticks:
+            finish()
+            for k in range(ticks - 1):
+                final(k)
+            break
         wait_for(turn.at[n, pl.ds(0, ncol - 1), slots(n)], t_recv.at[n])
         if n == 0:
             for k in range(1, ticks):
@@ -468,16 +494,21 @@
                 acc[later] = acc[later] - window_term(later, n - 1, solved)
         if n == 0:
             share_fold(cls == 3)
-            share_window(cls == 1)
+            share_window(cls < 2)
         if n == 1:
-            pass_on()
+            hand_over(range(4, 8))
+
+            @pl.when(zed > 0)
+            def _():
+                remote(win, wl.at[:, cls], wl_send, wl_recv.at[1], on_twin).start()
+
 
             @pl.when(zed > 0)
             def _():
                 settle()
 
-        if n >= 2:
-            final(n - 2)
+        if n == 3:
+            pass_on()
     final(ticks - 1)
 
     for d in range(1, LEVEL):
@@ -612,7 +643,7 @@
             dma,
             dma((LEVEL - 1,)),
             dma((ticks + 1,)),
-            dma((ticks + 1,)),
+            dma((ticks + 2,)),
             dma,
             dma((ticks,)),
             dma,

time: 88.2 us -> 85.5 us (0.969)
  Pallas kernels: 86.5 us -> 83.7 us
    pallas_call x1, Pallas kernels: 86.5 us -> 83.7 us  [per_device(): pl.pallas_call(functools.partial(kernel, nz, ncol), out_shape=jax.ShapeDt...]
where the time goes in v5:
time: 85.5 us; the launch traced here: 85.3 us
  Pallas kernels  83.7 us (98%)
  local copies, waits for them, and re-layouts  1.57 us (2%)
    pallas_call x1, Pallas kernels, per_device(): pl.pallas_call(functools.partial(kernel, nz, ncol), out_shape=jax.ShapeDt...  83.7 us

profile of v5, /device:TPU:1, one launch (start us, length us, event | category | flops | bytes accessed | tf_op | source)
XLA Modules:
  0.0 85.3 jit_solution(3406547180418478462)
XLA Ops:
  0.0 83.7 %shard_map.55 = f32[64,512]{1,0:T(8,128)} custom-call(f32[64,512]{1,0:T(8,128)} %bitcast.9, bf16[1024,1024]{1,0:T(8,128)(2,1)} %bitcast.5, bf16[1024,512]{1,0:T(8,128)(2,1)} %bitcast.6, bf16[4,64,1024]{2,1,0:T(8,128)(2,1)} %bitcast.7, bf16[4,64,1024]{2,1,0:T(8,128)(2,1)} %dinv_h.1), custom_call_target="tpu_custom_call" | custom-call | tf_op jit(solution)/shard_map/pallas_call | solution.py:591
  83.8 1.6 %copy.7 = f32[1,1,64,512]{3,2,1,0:T(8,128)} copy(f32[1,1,64,512]{3,2,1,0:T(8,128)} %bitcast.8) | data formatting | bytes 262144

commit v6 on v5

--- a/solution.py
+++ b/solution.py
@@ -232,24 +232,27 @@
     def _():
         send_x(range(begin, near))
 
-    @pl.when(active)
-    def _():
-        for c in range(ncol):
-
-            @pl.when((c >= lowest) & (col != c))
-            def _():
-                wait_for(ybuf.at[c], y_recv.at[c])
-
-            @pl.when(c < lowest)
-            def _():
-                ybuf[c] = jnp.zeros((rows, LANES), BF16)
-
-        tt[mine, group] = jnp.dot(
-            wc[mine, mine], ybuf[...].reshape(size, LANES), preferred_element_type=F32
-        ).astype(BF16)
-        for d in along_z:
-            part = tt.at[mine, group]
-            remote(part, part, tz_send, tz_recv, on_z(d)).start()
+    def fold_here(who):
+        @pl.when(active & who)
+        def _():
+            for c in range(ncol):
+
+                @pl.when((c >= lowest) & (col != c))
+                def _():
+                    wait_for(ybuf.at[c], y_recv.at[c])
+
+                @pl.when(c < lowest)
+                def _():
+                    ybuf[c] = jnp.zeros((rows, LANES), BF16)
+
+            tt[mine, group] = jnp.dot(
+                wc[mine, mine], ybuf[...].reshape(size, LANES), preferred_element_type=F32
+            ).astype(BF16)
+            for d in along_z:
+                part = tt.at[mine, group]
+                remote(part, part, tz_send, tz_recv, on_z(d)).start()
+
+    fold_here(zed > 0)
 
     beyond = lax.rem(cls + 2, LEVEL)
     twin = cls + 1 - 2 * lax.rem(cls, 2)
@@ -342,6 +345,7 @@
         return pin[k].astype(F32)
 
     deal(cls == 0)
+    fold_here(zed == 0)
 
     @pl.when((zed == 0) & carrier)
     def _():

time: 85.5 us -> 84.9 us (level)
  no operation moved by 1% of the time
where the time goes in v6:
time: 84.9 us; the launch traced here: 84.8 us
  Pallas kernels  83.2 us (98%)
  local copies, waits for them, and re-layouts  1.57 us (2%)
    pallas_call x1, Pallas kernels, per_device(): pl.pallas_call(functools.partial(kernel, nz, ncol), out_shape=jax.ShapeDt...  83.2 us

profile of v6, /device:TPU:1, one launch (start us, length us, event | category | flops | bytes accessed | tf_op | source)
XLA Modules:
  0.0 84.8 jit_solution(9078984661311883449)
XLA Ops:
  0.0 83.2 %shard_map.55 = f32[64,512]{1,0:T(8,128)} custom-call(f32[64,512]{1,0:T(8,128)} %bitcast.9, bf16[1024,1024]{1,0:T(8,128)(2,1)} %bitcast.5, bf16[1024,512]{1,0:T(8,128)(2,1)} %bitcast.6, bf16[4,64,1024]{2,1,0:T(8,128)(2,1)} %bitcast.7, bf16[4,64,1024]{2,1,0:T(8,128)(2,1)} %dinv_h.1), custom_call_target="tpu_custom_call" | custom-call | tf_op jit(solution)/shard_map/pallas_call | solution.py:595
  83.2 1.6 %copy.7 = f32[1,1,64,512]{3,2,1,0:T(8,128)} copy(f32[1,1,64,512]{3,2,1,0:T(8,128)} %bitcast.8) | data formatting | bytes 262144

commit v7 on v6

--- a/solution.py
+++ b/solution.py
@@ -656,7 +656,7 @@
         compiler_params=pltpu.CompilerParams(
             collective_id=0,
             has_side_effects=True,
-            vmem_limit_bytes=60 * 1024 * 1024,
+            vmem_limit_bytes=55040 * 1024,
         ),
     )(
         right_side.reshape(rows, columns),

time: 84.9 us -> 83.3 us (0.981)
  local copies, waits for them, and re-layouts: 1.57 us -> 0.66 us
    unnamed x1, local copies, waits for them, and re-layouts: 1.57 us -> 0.66 us
where the time goes in v7:
time: 83.3 us; the launch traced here: 83.2 us
  Pallas kernels  82.6 us (99%)
    pallas_call x1, Pallas kernels, per_device(): pl.pallas_call(functools.partial(kernel, nz, ncol), out_shape=jax.ShapeDt...  82.6 us

profile of v7, /device:TPU:1, one launch (start us, length us, event | category | flops | bytes accessed | tf_op | source)
XLA Modules:
  0.0 83.2 jit_solution(15418109012557234355)
XLA Ops:
  0.0 82.6 %shard_map.55 = f32[64,512]{1,0:T(8,128)S(1)} custom-call(f32[64,512]{1,0:T(8,128)} %bitcast.9, bf16[1024,1024]{1,0:T(8,128)(2,1)} %bitcast.6, bf16[1024,512]{1,0:T(8,128)(2,1)} %bitcast.7, bf16[4,64,1024]{2,1,0:T(8,128)(2,1)} %bitcast.8, bf16[4,64,1024]{2,1,0:T(8,128)(2,1)} %dinv_h.1), custom_call_target="tpu_custom_call" | custom-call | tf_op jit(solution)/shard_map/pallas_call | solution.py:595
  82.6 0.7 copy.7
